TPU v7x, 128 devices: a whole 4x4x4 slice. The times are simulated.
128 devices in a mesh: ctx: 32 (over x, y, core), row: 4 (over z).
Axes of the slice: x: 4, y: 4, z: 4, core: 2. Of those that a mesh axis runs over, the one named last changes fastest.
Arguments:
- queries: bfloat16 [32, 2, 384, 1024], P('ctx', None, 'row'), may hold values from -110 to 110
- keys: bfloat16 [32, 2, 384, 128], P('ctx', None, 'row'), may hold values from -5 to 5
- values: bfloat16 [32, 2, 384, 128], P('ctx', None, 'row'), may hold values from -6 to 6
- assignment: int32 [32, 2], replicated, may hold values from 0 to 63, as said below
Outputs:
- attended: bfloat16 [32, 2, 384, 1024], P('ctx', None, 'row')
- log_total: float32 [32, 2, 8, 384], P('ctx', None, None, 'row')
Inputs may be any that keep to these rules, and one draw needn't show every extreme that they name: Every span number 0 to 63 stands exactly once in assignment.
All inputs are finite; a program needn't handle non-finite values.
Results may differ from a plain program's by a relative error of at most 0.017.
Values may be sent and summed in bfloat16 or wider, within the bound.
No kernel may reach another device: no remote copies, remote signals or barrier semaphores. Data moves between devices by JAX's collectives and lax.ppermute only.
A program may use at most 64 MiB of HBM per device.

v0:
```python
import functools
import itertools

import jax
import jax.numpy as jnp
from jax import lax
from jax.experimental import pallas as pl
from jax.experimental.pallas import tpu as pltpu
from jax.sharding import PartitionSpec as P

BF, F32, I32 = jnp.bfloat16, jnp.float32, jnp.int32
NX, NY, NC, NZ = 4, 4, 2, 4
HEADS, HD, SPAN = 8, 128, 384
ROWS = SPAN // NZ
HALF = ROWS // 2
TQ = HEADS * ROWS
NK = NY * NC * 2
MAX_STEPS = 8 * NK // 2 + 8
NEG = -1e30
MAX_RISE = 100.0
SCALE = 1.4426950408889634 / HD**0.5
LN2 = 0.6931471805599453


def device(x, y, core, z):
    return ((x * NY + y) * NC + core) * NZ + z


def permute(a, target):
    places = itertools.product(range(NX), range(NY), range(NC), range(NZ))
    return lax.ppermute(a, ("ctx", "row"), [(device(*p), device(*target(*p))) for p in places])


def shift_x(a, d):
    return permute(a, lambda x, y, core, z: ((x + d) % NX, y, core, z))


def shift_plane(a, d, phase):
    def target(x, y, core, z):
        return (x, (y + d) % NY, core, z) if core == phase else (x, y, core, (z + d) % NZ)

    return permute(a, target)


def swap_core(a):
    return permute(a, lambda x, y, core, z: (x, y, 1 - core, z))


def dot_t(a, b):
    return lax.dot_general(a, b, (((1,), (1,)), ((), ())), preferred_element_type=F32)


def dot(a, b):
    return lax.dot_general(a, b, (((1,), (0,)), ((), ())), preferred_element_type=F32)


REL = (0, -1, 1, 2)


def gather_line(a):
    return jnp.stack([a, shift_plane(a, 1, 0), shift_plane(a, -1, 0), shift_plane(a, 2, 0)])


def gather_plane(line):
    return line, shift_plane(line, 1, 1), shift_plane(line, -1, 1)


def gather_far(low, high):
    return shift_plane(low[:2], 1, 1), shift_plane(high[2:], -1, 1)


def place():
    ctx = lax.axis_index("ctx")
    return ctx // (NY * NC), ctx // NC % NY, ctx % NC, lax.axis_index("row")


def arrange_kernel(at, table, line, low, high, far_0, far_1, out_ref, vals):
    y, core, z = at[1], at[2], at[3]
    here_1, here_2 = jnp.where(core == 0, y, z), jnp.where(core == 0, z, y)
    for i, di in enumerate(REL):
        for j, dj in enumerate(REL):
            one, two = lax.rem(here_1 + di + 4, 4), lax.rem(here_2 + dj + 4, 4)
            span, part = jnp.where(core == 0, one, two) * 2, jnp.where(core == 0, two, one)
            at_row = pl.multiple_of(part * ROWS, 16)
            source = (line.at[i], low.at[i], high.at[i], (far_0, far_1)[i // 2].at[i % 2])[j]
            for slot in range(2):
                out_ref[span + slot, pl.ds(at_row, ROWS), :] = source[slot, :, :HD]
                vals[span + slot, pl.ds(at_row, ROWS), :] = source[slot, :, HD:]

    def turn(span, _):
        for b in range(3):
            block = vals[span, b * 128 : (b + 1) * 128, :]
            out_ref[span, SPAN + b * 128 : SPAN + (b + 1) * 128, :] = block.astype(F32).T.astype(BF)
        return 0

    lax.fori_loop(0, 2 * NY, turn, 0)


def arrange(at, table, parts):
    vmem = pl.BlockSpec(memory_space=pltpu.VMEM)
    return pl.pallas_call(
        arrange_kernel,
        out_shape=jax.ShapeDtypeStruct((2 * NY, 2 * SPAN, HD), BF),
        in_specs=[pl.BlockSpec(memory_space=pltpu.SMEM)] * 2 + [vmem] * 5,
        out_specs=vmem,
        scratch_shapes=[pltpu.VMEM((2 * NY, SPAN, HD), BF)],
        compiler_params=pltpu.CompilerParams(vmem_limit_bytes=40 << 20),
        name="arrange",
    )(at, table, *parts)


def attend_kernel(q0, slots, diagonal, table, *refs):
    nq, groups = len(slots), len(slots) // 2
    n_in = 1 + max(array for array, _ in slots)
    queries, (kv_own, kv_other), outs = refs[:n_in], refs[n_in : n_in + 2], refs[n_in + 2 : n_in + 2 + groups]
    kv, raw, qt, s0, s1, p0, p1, t0, t1, acc, ms, starts, sems = refs[n_in + 2 + groups :]
    fetches = [
        pltpu.make_async_copy(queries[array].at[0, slot], raw.at[t], sems.at[2 + t])
        for t, (array, slot) in enumerate(slots)
    ]
    copies = [
        pltpu.make_async_copy(kv_own, kv.at[: NK // 2], sems.at[0]),
        pltpu.make_async_copy(kv_other, kv.at[NK // 2 :], sems.at[1]),
    ]
    for c in fetches + copies:
        c.start()
    for t in range(nq):
        fetches[t].wait()
        full = raw[t].astype(F32) * SCALE
        high = full.astype(BF)
        low = (full - high.astype(F32)).astype(BF)
        for h in range(HEADS):
            rows, cols = slice(h * ROWS, (h + 1) * ROWS), slice(h * HD, (h + 1) * HD)
            qt[t, rows, :HD] = high[:, cols]
            qt[t, rows, HD:] = low[:, cols]
    base = table[6, q0]
    steps = table[6, q0 + nq] - base
    for c in copies:
        c.wait()

    def entry(row, i):
        return table[row, base + jnp.clip(i, 0, jnp.maximum(steps - 1, 0))]

    def tile_of(i):
        return jnp.where(jnp.logical_and(i >= 0, i < steps), entry(0, i) - q0, nq)

    def spans_of(i):
        return [jnp.clip(entry(1 + half, i), 0, NK - 1) for half in range(2)]

    def key_rows(i):
        k = jnp.concatenate([kv[k, :SPAN, :] for k in spans_of(i)], axis=0)
        return jnp.concatenate([k, k], axis=1)

    def value_rows(*spans):
        blocks = [kv[k, SPAN + b * HD : SPAN + (b + 1) * HD, :] for k in spans for b in range(3)]
        return jnp.concatenate([jnp.concatenate(blocks, axis=1), jnp.ones((16, SPAN * len(spans)), BF)], axis=0)

    def query_tile(i):
        return jnp.clip(entry(0, i) - q0, 0, nq - 1)

    def clear():
        acc[...] = jnp.zeros_like(acc)
        ms[...] = jnp.full_like(ms, NEG)
        p1[...] = jnp.zeros_like(p1)

    def column_tops(x):
        return [jnp.max(x[half * SPAN : (half + 1) * SPAN], axis=0, keepdims=True) for half in range(2)]

    def last_product(i, p, rescale):
        tile = tile_of(i)
        acc[tile] = acc[tile] * rescale + dot(value_rows(*spans_of(i)), p[...])

    def quick_step(i, p_in, p_out, carry):
        base_top, top, rescale, rise = carry
        first, pad = entry(3, i) == 1, entry(5, i) == 1
        ref = jnp.where(first, starts[query_tile(i)], top)
        tops = (ref, jnp.where(pad, -NEG, ref))
        q, k = qt.at[query_tile(i)], key_rows(i)
        v, tile = value_rows(*spans_of(i - 1)), tile_of(i - 1)
        seen = []
        for c in range(0, TQ, 256):
            cols = slice(c, c + 256)
            acc[tile, :, cols] = acc[tile, :, cols] * rescale[:, cols] + dot(v, p_in[:, cols])
            x = dot_t(k, q[cols, :])
            for half in range(2):
                rows = slice(half * SPAN, (half + 1) * SPAN)
                p_out[rows, cols] = jnp.exp2(x[rows] - tops[half][:, cols]).astype(BF)
            high, low = column_tops(x)
            seen.append(jnp.maximum(high, jnp.where(pad, NEG, low)))
        ms[tile_of(i)] = ref
        new = jnp.concatenate(seen, axis=1)
        rescale = jnp.where(first, 0.0, jnp.exp2(base_top - ref))
        return ref, jnp.maximum(ref, new), rescale, jnp.maximum(rise, new - ref)

    def quick_pair(ii, carry):
        carry = quick_step(2 * ii, p1, p0, carry)
        return quick_step(2 * ii + 1, p0, p1, carry)

    def safe_step(i, s_in, s_out, t_in, t_out, p_in, p_out, carry):
        m, rescale = carry
        first, pad = entry(3, i) == 1, entry(5, i) == 1
        m = jnp.where(first, NEG, m)
        new = jnp.maximum(jnp.maximum(m, t_in[0:1, :]), jnp.where(pad, NEG, t_in[1:2, :]))
        tops = (new, jnp.where(pad, -NEG, new))
        q, k = qt.at[query_tile(i + 1)], key_rows(i + 1)
        v, tile = value_rows(*spans_of(i - 1)), tile_of(i - 1)
        for c in range(0, TQ, 256):
            cols = slice(c, c + 256)
            for half in range(2):
                rows = slice(half * SPAN, (half + 1) * SPAN)
                p_out[rows, cols] = jnp.exp2(s_in[rows, cols] - tops[half][:, cols]).astype(BF)
            acc[tile, :, cols] = acc[tile, :, cols] * rescale[:, cols] + dot(v, p_in[:, cols])
            x = dot_t(k, q[cols, :])
            s_out[:, cols] = x
            t_out[0:1, cols], t_out[1:2, cols] = column_tops(x)
        ms[tile_of(i)] = new
        return new, jnp.exp2(m - new)

    def safe_pair(ii, carry):
        carry = safe_step(2 * ii, s0, s1, t0, t1, p1, p0, carry)
        return safe_step(2 * ii + 1, s1, s0, t1, t0, p0, p1, carry)

    row = jnp.zeros((1, TQ), F32)
    pairs = (steps + 1) // 2
    clear()
    for t in range(nq):
        k = kv[jnp.clip(table[1, table[6, q0 + t]], 0, NK - 1), :HD, :]
        x = dot_t(jnp.concatenate([k, k], axis=1), qt[t])
        starts[t] = jnp.max(x, axis=0, keepdims=True)
    carry = lax.fori_loop(0, steps // 2, quick_pair, (row, row, row, row))

    def odd_end(carry):
        carry = quick_step(steps - 1, p1, p0, carry)
        last_product(steps - 1, p0, carry[2])
        return carry[3]

    def even_end(carry):
        last_product(steps - 1, p1, carry[2])
        return carry[3]

    rise = lax.cond(steps % 2 == 1, odd_end, even_end, carry)

    @pl.when(jnp.logical_not(jnp.max(rise) <= MAX_RISE))
    def _():
        clear()
        x = dot_t(key_rows(0), qt[query_tile(0)])
        s0[...] = x
        t0[0:1, :], t0[1:2, :] = column_tops(x)
        _, rescale = lax.fori_loop(0, pairs, safe_pair, (row + NEG, row + 1.0))
        last_product(2 * pairs - 1, p1, rescale)

    if diagonal:
        key = lax.broadcasted_iota(I32, (SPAN, TQ), 0)
        query = lax.rem(lax.broadcasted_iota(I32, (SPAN, TQ), 1), ROWS) + table[6, 9] * ROWS
        seen = key <= query
        for slot, (s, p) in enumerate(((s0, p0), (s1, p1))):
            k = kv[table[6, 10] + slot, :SPAN, :]
            x = jnp.where(seen, dot_t(jnp.concatenate([k, k], axis=1), qt[slot]), NEG)
            s[:SPAN, :] = x
            new = jnp.maximum(ms[slot], jnp.max(x, axis=0, keepdims=True))
            rescale = jnp.exp2(ms[slot] - new)
            w = jnp.exp2(s[:SPAN, :] - new)
            ms[slot] = new
            v = value_rows(table[6, 10] + slot)
            acc[slot] = acc[slot] * rescale + dot(v, w.astype(BF))
    for tile in range(nq):
        total = acc[tile, HD : HD + 1, :]
        any_seen = total > 0.0
        safe = jnp.where(any_seen, total, 1.0)
        out = outs[tile // 2]
        out[tile % 2, :HD, :] = (acc[tile, :HD, :] * (1.0 / safe)).astype(BF)
        left = jnp.broadcast_to(jnp.where(any_seen, ms[tile] * LN2 + jnp.log(safe), NEG), (16, TQ))
        for part in range(3):
            rounded = left.astype(BF)
            out[tile % 2, HD + 16 * part : HD + 16 * part + 16, :] = rounded
            left = left - rounded.astype(F32)


def attend(q0, slots, diagonal, table, queries, kv_own, kv_other):
    groups = len(slots) // 2
    vmem = pl.BlockSpec(memory_space=pltpu.VMEM)
    hbm = pl.BlockSpec(memory_space=pl.ANY)
    tile = 2 * SPAN
    flops = 2 * groups * TQ * NK * SPAN * HD * 2
    return pl.pallas_call(
        functools.partial(attend_kernel, q0, slots, diagonal),
        out_shape=[jax.ShapeDtypeStruct((2, HD + 48, TQ), BF)] * groups,
        in_specs=[pl.BlockSpec(memory_space=pltpu.SMEM)] + [hbm] * (len(queries) + 2),
        out_specs=[vmem] * groups,
        scratch_shapes=[
            pltpu.VMEM((NK, 2 * SPAN, HD), BF),
            pltpu.VMEM((2 * groups, ROWS, HEADS * HD), BF),
            pltpu.VMEM((2 * groups, TQ, 2 * HD), BF),
            pltpu.VMEM((tile, TQ), F32),
            pltpu.VMEM((tile, TQ), F32),
            pltpu.VMEM((tile, TQ), BF),
            pltpu.VMEM((tile, TQ), BF),
            pltpu.VMEM((8, TQ), F32),
            pltpu.VMEM((8, TQ), F32),
            pltpu.VMEM((2 * groups + 1, HD + 16, TQ), F32),
            pltpu.VMEM((2 * groups + 1, 1, TQ), F32),
            pltpu.VMEM((2 * groups, 1, TQ), F32),
            pltpu.SemaphoreType.DMA((2 + 2 * groups,)),
        ],
        compiler_params=pltpu.CompilerParams(vmem_limit_bytes=26 << 20),
        cost_estimate=pl.CostEstimate(flops=flops, bytes_accessed=6 << 20, transcendentals=flops // 512),
        name="attend",
    )(table, *queries, kv_own, kv_other)


def combine_kernel(*refs):
    parts, (out_ref, lse_ref) = refs[:4], refs[4:]
    for slot in range(2):
        logs = [sum(r[slot, HD + 16 * p : HD + 16 * p + 1, :].astype(F32) for p in range(3)) for r in parts]
        top = functools.reduce(jnp.maximum, logs)
        raw = [jnp.exp(v - top) for v in logs]
        total = sum(raw)
        lse = top + jnp.log(total)
        mixed = sum((w / total) * r[slot, :HD, :].astype(F32) for w, r in zip(raw, parts)).T
        for h in range(HEADS):
            rows = slice(h * ROWS, (h + 1) * ROWS)
            out_ref[0, slot, :, h * HD : (h + 1) * HD] = mixed[rows].astype(BF)
            lse_ref[0, slot, h : h + 1, :] = lse[:, rows]


def combine(parts):
    vmem = pl.BlockSpec(memory_space=pltpu.VMEM)
    return pl.pallas_call(
        combine_kernel,
        out_shape=(
            jax.ShapeDtypeStruct((1, 2, ROWS, HEADS * HD), BF),
            jax.ShapeDtypeStruct((1, 2, HEADS, ROWS), F32),
        ),
        in_specs=[vmem] * 4,
        out_specs=(vmem, vmem),
        compiler_params=pltpu.CompilerParams(vmem_limit_bytes=32 << 20),
        name="combine",
    )(*parts)


ORDER = (2, -1, 1, 0)


def plan_kernel(at, assignment, table, order):
    x, y, core, row = at[0], at[1], at[2], at[3]
    keys = [
        assignment[(x * NY + i) * NC + c, slot] for c in (core, 1 - core) for i in range(NY) for slot in range(2)
    ]
    for i, key in enumerate(keys):
        order[sum((other < key).astype(I32) for other in keys)] = i
    begin = jnp.int32(0)
    for t in range(8):
        source = lax.rem(x + ORDER[t // 2] + NX, NX)
        query = assignment[(source * NY + y) * NC + core, t % 2]
        count = sum((key < query).astype(I32) for key in keys)
        tiles = lax.div(count + 1, 2)
        table[6, t] = begin

        def write(j, _):
            at_step = begin + j
            last = (j == tiles - 1).astype(I32)
            table[0, at_step] = t
            table[1, at_step] = order[2 * j]
            table[2, at_step] = order[2 * j + 1]
            table[3, at_step] = (j == 0).astype(I32)
            table[4, at_step] = last
            table[5, at_step] = last * lax.rem(count, 2)
            return 0

        lax.fori_loop(0, tiles, write, 0)
        begin = begin + tiles
    table[6, 8] = begin
    table[6, 9] = row
    table[6, 10] = y * 2


def plan(at, assignment):
    smem = pl.BlockSpec(memory_space=pltpu.SMEM)
    return pl.pallas_call(
        plan_kernel,
        out_shape=jax.ShapeDtypeStruct((8, MAX_STEPS), I32),
        in_specs=[smem, smem],
        out_specs=smem,
        scratch_shapes=[pltpu.SMEM((NK,), I32)],
        name="plan",
    )(at, assignment)


def local(queries, keys, values, assignment):
    at = jnp.stack(place()).astype(I32)
    table = plan(at, assignment)
    near = gather_line(jnp.concatenate([keys[0], values[0]], axis=-1))
    near, queries_next = lax.optimization_barrier((near, queries))
    line, low, high = gather_plane(near)
    from_low, from_high = shift_x(queries_next, 1), shift_x(queries_next, -1)
    far = shift_plane(line, 2, 1)
    kv_own = arrange(at, table, (line, low, high, far[:2], far[2:]))
    kv_own, from_low, from_high = lax.optimization_barrier((kv_own, from_low, from_high))
    kv_other = swap_core(kv_own)
    from_far = shift_x(from_low[:, :1], 1), shift_x(from_high[:, 1:], -1)
    kv = kv_own, kv_other
    both = ((0, 0), (0, 1))
    (far,) = attend(0, ((0, 0), (1, 0)), False, table, from_far, *kv)
    far = shift_x(far, 2)
    low, high = attend(2, both + ((1, 0), (1, 1)), False, table, (from_low, from_high), *kv)
    low, high = shift_x(low, -1), shift_x(high, 1)
    (own,) = attend(6, both, True, table, (queries,), *kv)
    return combine([own, low, high, far])


def solution(mesh):
    in_specs = (
        P("ctx", None, "row", None),
        P("ctx", None, "row", None),
        P("ctx", None, "row", None),
        P(),
    )
    out_specs = (P("ctx", None, "row", None), P("ctx", None, None, "row"))
    return jax.shard_map(local, mesh=mesh, in_specs=in_specs, out_specs=out_specs, check_vma=False)
```

profile of v0, /device:TPU:0, one launch (start us, length us, event | category | flops | bytes accessed | tf_op | source)
XLA Modules:
  0.0 80.9 jit_solution(1779023135787245330)
XLA Ops:
  0.6 0.8 %fusion = (bf16[1,2,96,256]{3,2,1,0:T(8,128)(2,1)S(1)}, bf16[2,96,256]{2,1,0:T(8,128)(2,1)S(1)}) fusion(bf16[2,96,128]{2,1,0:T(8,128)(2,1)} %bitcast.14, bf16[2,96,128]{2,1,0:T(8,128)(2,1)} %bitcast.15), kind=kLoop, calls=%fused_computation.3 | loop fusion | flops 196608 | bytes 294912 | tf_op jit(solution)/shard_map/stack | solution.py:61
  1.5 3.2 %collective-permute-start.1 = (bf16[2,96,256]{2,1,0:T(8,128)(2,1)S(1)}, bf16[2,96,256]{2,1,0:T(8,128)(2,1)S(1)}, u32[]{:S(2)}, u32[]{:S(2)}) collective-permute-start(bf16[2,96,256]{2,1,0:T(8,128)(2,1)S(1)} %get-tuple-element.19), channel_id=1, source_target_pairs={{0,24},{1,25},{2,26},{3,27},{4,7},{5,4},{6,5},{7,6},{8,0},{9,1},{1... | collective-permute-start | bytes 294920 | tf_op jit(solution)/shard_map/ppermute | solution.py:31
  4.6 0.0 collective-permute-start
  4.6 2.2 %collective-permute-start.2 = (bf16[2,96,256]{2,1,0:T(8,128)(2,1)S(1)}, bf16[2,96,256]{2,1,0:T(8,128)(2,1)S(1)}, u32[]{:S(2)}, u32[]{:S(2)}) collective-permute-start(bf16[2,96,256]{2,1,0:T(8,128)(2,1)S(1)} %get-tuple-element.19), channel_id=1, source_target_pairs={{0,16},{1,17},{2,18},{3,19},{4,6},{5,7},{6,4},{7,5},{8,24},{9,25},... | collective-permute-start | bytes 294920 | tf_op jit(solution)/shard_map/ppermute | solution.py:31
  6.8 0.0 collective-permute-done.1
  6.9 4.7 %collective-permute-done = bf16[2,96,256]{2,1,0:T(8,128)(2,1)S(1)} collective-permute-done((bf16[2,96,256]{2,1,0:T(8,128)(2,1)S(1)}, bf16[2,96,256]{2,1,0:T(8,128)(2,1)S(1)}, u32[]{:S(2)}, u32[]{:S(2)}) %collective-permute-start) | collective-permute-done | bytes 98336 | tf_op jit(solution)/shard_map/ppermute | solution.py:31
  11.5 0.1 pad_maximum_fusion.line
  11.6 4.0 %collective-permute-start.5 = (bf16[4,2,96,256]{3,2,1,0:T(8,128)(2,1)S(1)}, bf16[4,2,96,256]{3,2,1,0:T(8,128)(2,1)S(1)}, u32[]{:S(2)}, u32[]{:S(2)}) collective-permute-start(bf16[4,2,96,256]{3,2,1,0:T(8,128)(2,1)S(1)} %pad_maximum_fusion.line), channel_id=1, source_target_pairs={{0,2},{1,3},{2,0},{3,1},{4,20},{5,21},{6,22},{7,23},{8,10},{9,11},... | collective-permute-start | bytes 1179656 | tf_op jit(solution)/shard_map/ppermute | solution.py:31
  15.5 0.7 collective-permute-start.4
  16.2 1.3 %collective-permute-start.3 = (bf16[4,2,96,256]{3,2,1,0:T(8,128)(2,1)S(1)}, bf16[4,2,96,256]{3,2,1,0:T(8,128)(2,1)S(1)}, u32[]{:S(2)}, u32[]{:S(2)}) collective-permute-start(bf16[4,2,96,256]{3,2,1,0:T(8,128)(2,1)S(1)} %pad_maximum_fusion.line), channel_id=1, source_target_pairs={{0,1},{1,2},{2,3},{3,0},{4,12},{5,13},{6,14},{7,15},{8,9},{9,10},{... | collective-permute-start | bytes 1179656 | tf_op jit(solution)/shard_map/ppermute | solution.py:31
  17.6 2.8 %collective-permute-start.7 = (bf16[1,2,96,1024]{3,2,1,0:T(8,128)(2,1)}, bf16[1,2,96,1024]{3,2,1,0:T(8,128)(2,1)S(1)}, u32[]{:S(2)}, u32[]{:S(2)}) collective-permute-start(bf16[1,2,96,1024]{3,2,1,0:T(8,128)(2,1)} %refs_0_.1), channel_id=1, source_target_pairs={{0,96},{1,97},{2,98},{3,99},{4,100},{5,101},{6,102},{7,103},{8,104... | collective-permute-start | bytes 1179656 | tf_op jit(solution)/shard_map/ppermute | solution.py:31
  20.3 1.4 %copy.6.assignment = s32[32,2]{1,0:T(8,128)} copy(s32[32,2]{0,1:T(2,128)} %param.7) | data formatting | bytes 512 | tf_op args[3]
  21.7 0.6 pad_add_fusion.at
  22.3 2.5 %plan.1.table = s32[8,72]{1,0:T(8,128)} custom-call(s32[4]{0:T(128)} %pad_add_fusion.at, s32[32,2]{1,0:T(8,128)} %copy.6.assignment), custom_call_target="tpu_custom_call" | custom-call | tf_op jit(solution)/shard_map/plan/pallas_call | solution.py:379
  24.8 0.0 collective-permute-done.5
  24.8 1.7 %collective-permute-done.4.high = bf16[4,2,96,256]{3,2,1,0:T(8,128)(2,1)S(1)} collective-permute-done((bf16[4,2,96,256]{3,2,1,0:T(8,128)(2,1)S(1)}, bf16[4,2,96,256]{3,2,1,0:T(8,128)(2,1)S(1)}, u32[]{:S(2)}, u32[]{:S(2)}) %collective-permute-start.4) | collective-permute-done | bytes 393248 | tf_op jit(solution)/shard_map/ppermute | solution.py:31
  26.6 0.0 collective-permute-done.3.low
  26.6 0.7 copy-done
  27.3 0.6 copy-done.1
  27.9 1.8 %arrange.1.refs_1_.refs_2_ = bf16[8,768,128]{2,1,0:T(8,128)(2,1)S(1)} custom-call(s32[4]{0:T(128)S(1)} %copy-done.1, s32[8,72]{1,0:T(8,128)S(1)} %copy-done, bf16[4,2,96,256]{3,2,1,0:T(8,128)(2,1)S(1)} %pad_maximum_fusion.line, bf16[4,2,96,256]{3,2,1,0:T(8,128)(2,1)S(1)} %collective-permute-done.3.low, ...), custom_call_target="tpu_custom_call" | custom-call | tf_op jit(solution)/shard_map/arrange/pallas_call | solution.py:101
  29.7 0.7 collective-permute-done.6.refs_0_
  30.4 2.2 %collective-permute-start.12 = (bf16[1,1,96,1024]{3,2,1,0:T(8,128)(2,1)S(1)}, bf16[1,1,96,1024]{3,2,1,0:T(8,128)(2,1)S(1)}, u32[]{:S(2)}, u32[]{:S(2)}) collective-permute-start(bf16[1,1,96,1024]{3,2,1,0:T(8,128)(2,1)S(1)} %slice.15), channel_id=1, source_target_pairs={{0,96},{1,97},{2,98},{3,99},{4,100},{5,101},{6,102},{7,103},{8,104... | collective-permute-start | bytes 589832 | tf_op jit(solution)/shard_map/ppermute | solution.py:31
  32.7 1.1 %collective-permute-done.8.refs_2_.refs_3_ = bf16[8,768,128]{2,1,0:T(8,128)(2,1)S(1)} collective-permute-done((bf16[8,768,128]{2,1,0:T(8,128)(2,1)S(1)}, bf16[8,768,128]{2,1,0:T(8,128)(2,1)S(1)}, u32[]{:S(2)}, u32[]{:S(2)}) %collective-permute-start.8) | collective-permute-done | bytes 1572896 | tf_op jit(solution)/shard_map/ppermute | solution.py:31
  33.8 15.6 %attend.4 = (bf16[2,176,768]{2,1,0:T(8,128)(2,1)S(1)}, bf16[2,176,768]{2,1,0:T(8,128)(2,1)S(1)}) custom-call(s32[8,72]{1,0:T(8,128)S(1)} %copy-done, bf16[1,2,96,1024]{3,2,1,0:T(8,128)(2,1)S(1)} %collective-permute-done.6.refs_0_, bf16[1,2,96,1024]{3,2,1,0:T(8,128)(2,1)S(1)} %collective-permute-done.7.refs_1_, ...), custom_call_target="tpu_custom_call" | custom-call | flops 4831838208 | bytes 6291456 | tf_op jit(solution)/shard_map/attend/pallas_call | solution.py:285
  49.4 0.1 collective-permute-start.9
  49.5 0.0 copy-start.2
  49.5 2.0 %collective-permute-start.10 = (bf16[2,176,768]{2,1,0:T(8,128)(2,1)S(1)}, bf16[2,176,768]{2,1,0:T(8,128)(2,1)S(1)}, u32[]{:S(2)}, u32[]{:S(2)}) collective-permute-start(bf16[2,176,768]{2,1,0:T(8,128)(2,1)S(1)} %get-tuple-element.15), channel_id=1, source_target_pairs={{0,32},{1,33},{2,34},{3,35},{4,36},{5,37},{6,38},{7,39},{8,40},{9,... | collective-permute-start | bytes 1622024 | tf_op jit(solution)/shard_map/ppermute | solution.py:31
  51.5 5.0 %attend.5 = bf16[2,176,768]{2,1,0:T(8,128)(2,1)S(1)} custom-call(s32[8,72]{1,0:T(8,128)S(1)} %copy-done, bf16[1,1,96,1024]{3,2,1,0:T(8,128)(2,1)S(1)} %collective-permute-done.11.refs_0_, bf16[1,1,96,1024]{3,2,1,0:T(8,128)(2,1)S(1)} %collective-permute-done.12.refs_1_, bf16[8,768,128]{2,1,0:T(8,128)(2,1)S(1)} %arrange.1.refs_1_.refs_2_, ...), custom_call_target="tpu_custom_call" | custom-call | flops 2415919104 | bytes 6291456 | tf_op jit(solution)/shard_map/attend/pallas_call | solution.py:285
  56.5 8.4 %collective-permute-start.13 = (bf16[2,176,768]{2,1,0:T(8,128)(2,1)S(1)}, bf16[2,176,768]{2,1,0:T(8,128)(2,1)S(1)}, u32[]{:S(2)}, u32[]{:S(2)}) collective-permute-start(bf16[2,176,768]{2,1,0:T(8,128)(2,1)S(1)} %attend.5), channel_id=1, source_target_pairs={{0,64},{1,65},{2,66},{3,67},{4,68},{5,69},{6,70},{7,71},{8,72},{9,... | collective-permute-start | bytes 1622024 | tf_op jit(solution)/shard_map/ppermute | solution.py:31
  64.9 8.7 %attend.3.refs_0_ = bf16[2,176,768]{2,1,0:T(8,128)(2,1)S(1)} custom-call(s32[8,72]{1,0:T(8,128)S(1)} %copy-done, bf16[1,2,96,1024]{3,2,1,0:T(8,128)(2,1)S(1)} %copy-done.2, bf16[8,768,128]{2,1,0:T(8,128)(2,1)S(1)} %arrange.1.refs_1_.refs_2_, bf16[8,768,128]{2,1,0:T(8,128)(2,1)S(1)} %collective-permute-done.8.refs_2_.refs_3_), custom_call_target="tpu_custom_call" | custom-call | flops 2415919104 | bytes 6291456 | tf_op jit(solution)/shard_map/attend/pallas_call | solution.py:285
  73.6 6.1 %collective-permute-done.13.refs_3_ = bf16[2,176,768]{2,1,0:T(8,128)(2,1)S(1)} collective-permute-done((bf16[2,176,768]{2,1,0:T(8,128)(2,1)S(1)}, bf16[2,176,768]{2,1,0:T(8,128)(2,1)S(1)}, u32[]{:S(2)}, u32[]{:S(2)}) %collective-permute-start.13) | collective-permute-done | bytes 540704 | tf_op jit(solution)/shard_map/ppermute | solution.py:31
  79.7 1.2 %combine.1 = (bf16[1,2,96,1024]{3,2,1,0:T(8,128)(2,1)}, f32[1,2,8,96]{3,2,1,0:T(8,128)}) custom-call(bf16[2,176,768]{2,1,0:T(8,128)(2,1)S(1)} %attend.3.refs_0_, bf16[2,176,768]{2,1,0:T(8,128)(2,1)S(1)} %collective-permute-done.9.refs_1_, bf16[2,176,768]{2,1,0:T(8,128)(2,1)S(1)} %collective-permute-done.10.refs_2_, ...), custom_call_target="tpu_custom_call" | custom-call | tf_op jit(solution)/shard_map/combine/pallas_call | solution.py:328
  (15 shorter events, 0.1 us)
Async XLA Ops:
  1.5 5.4 %collective-permute-start.1 = (bf16[2,96,256]{2,1,0:T(8,128)(2,1)S(1)}, bf16[2,96,256]{2,1,0:T(8,128)(2,1)S(1)}, u32[]{:S(2)}, u32[]{:S(2)}) collective-permute-start(bf16[2,96,256]{2,1,0:T(8,128)(2,1)S(1)} %get-tuple-element.19), channel_id=1, source_target_pairs={{0,24},{1,25},{2,26},{3,27},{4,7},{5,4},{6,5},{7,6},{8,0},{9,1},{1... | collective-permute-start | bytes 294920 | tf_op jit(solution)/shard_map/ppermute | solution.py:31
  4.6 6.9 %collective-permute-start = (bf16[2,96,256]{2,1,0:T(8,128)(2,1)S(1)}, bf16[2,96,256]{2,1,0:T(8,128)(2,1)S(1)}, u32[]{:S(2)}, u32[]{:S(2)}) collective-permute-start(bf16[2,96,256]{2,1,0:T(8,128)(2,1)S(1)} %get-tuple-element.19), channel_id=1, source_target_pairs={{0,8},{1,9},{2,10},{3,11},{4,5},{5,6},{6,7},{7,4},{8,16},{9,17},{1... | collective-permute-start | bytes 294920 | tf_op jit(solution)/shard_map/ppermute | solution.py:31
  4.6 6.9 %collective-permute-start.2 = (bf16[2,96,256]{2,1,0:T(8,128)(2,1)S(1)}, bf16[2,96,256]{2,1,0:T(8,128)(2,1)S(1)}, u32[]{:S(2)}, u32[]{:S(2)}) collective-permute-start(bf16[2,96,256]{2,1,0:T(8,128)(2,1)S(1)} %get-tuple-element.19), channel_id=1, source_target_pairs={{0,16},{1,17},{2,18},{3,19},{4,6},{5,7},{6,4},{7,5},{8,24},{9,25},... | collective-permute-start | bytes 294920 | tf_op jit(solution)/shard_map/ppermute | solution.py:31
  11.6 13.2 %collective-permute-start.5 = (bf16[4,2,96,256]{3,2,1,0:T(8,128)(2,1)S(1)}, bf16[4,2,96,256]{3,2,1,0:T(8,128)(2,1)S(1)}, u32[]{:S(2)}, u32[]{:S(2)}) collective-permute-start(bf16[4,2,96,256]{3,2,1,0:T(8,128)(2,1)S(1)} %pad_maximum_fusion.line), channel_id=1, source_target_pairs={{0,2},{1,3},{2,0},{3,1},{4,20},{5,21},{6,22},{7,23},{8,10},{9,11},... | collective-permute-start | bytes 1179656 | tf_op jit(solution)/shard_map/ppermute | solution.py:31
  15.5 11.0 %collective-permute-start.4 = (bf16[4,2,96,256]{3,2,1,0:T(8,128)(2,1)S(1)}, bf16[4,2,96,256]{3,2,1,0:T(8,128)(2,1)S(1)}, u32[]{:S(2)}, u32[]{:S(2)}) collective-permute-start(bf16[4,2,96,256]{3,2,1,0:T(8,128)(2,1)S(1)} %pad_maximum_fusion.line), channel_id=1, source_target_pairs={{0,3},{1,0},{2,1},{3,2},{4,28},{5,29},{6,30},{7,31},{8,11},{9,8},{... | collective-permute-start | bytes 1179656 | tf_op jit(solution)/shard_map/ppermute | solution.py:31
  16.2 10.3 %collective-permute-start.3 = (bf16[4,2,96,256]{3,2,1,0:T(8,128)(2,1)S(1)}, bf16[4,2,96,256]{3,2,1,0:T(8,128)(2,1)S(1)}, u32[]{:S(2)}, u32[]{:S(2)}) collective-permute-start(bf16[4,2,96,256]{3,2,1,0:T(8,128)(2,1)S(1)} %pad_maximum_fusion.line), channel_id=1, source_target_pairs={{0,1},{1,2},{2,3},{3,0},{4,12},{5,13},{6,14},{7,15},{8,9},{9,10},{... | collective-permute-start | bytes 1179656 | tf_op jit(solution)/shard_map/ppermute | solution.py:31
  17.6 12.1 %collective-permute-start.7 = (bf16[1,2,96,1024]{3,2,1,0:T(8,128)(2,1)}, bf16[1,2,96,1024]{3,2,1,0:T(8,128)(2,1)S(1)}, u32[]{:S(2)}, u32[]{:S(2)}) collective-permute-start(bf16[1,2,96,1024]{3,2,1,0:T(8,128)(2,1)} %refs_0_.1), channel_id=1, source_target_pairs={{0,96},{1,97},{2,98},{3,99},{4,100},{5,101},{6,102},{7,103},{8,104... | collective-permute-start | bytes 1179656 | tf_op jit(solution)/shard_map/ppermute | solution.py:31
  20.3 10.1 %collective-permute-start.6 = (bf16[1,2,96,1024]{3,2,1,0:T(8,128)(2,1)}, bf16[1,2,96,1024]{3,2,1,0:T(8,128)(2,1)S(1)}, u32[]{:S(2)}, u32[]{:S(2)}) collective-permute-start(bf16[1,2,96,1024]{3,2,1,0:T(8,128)(2,1)} %refs_0_.1), channel_id=1, source_target_pairs={{0,32},{1,33},{2,34},{3,35},{4,36},{5,37},{6,38},{7,39},{8,40},{9,... | collective-permute-start | bytes 1179656 | tf_op jit(solution)/shard_map/ppermute | solution.py:31
  26.6 0.7 copy-start
  27.3 0.6 copy-start.1
  30.4 3.4 %collective-permute-start.8 = (bf16[8,768,128]{2,1,0:T(8,128)(2,1)S(1)}, bf16[8,768,128]{2,1,0:T(8,128)(2,1)S(1)}, u32[]{:S(2)}, u32[]{:S(2)}) collective-permute-start(bf16[8,768,128]{2,1,0:T(8,128)(2,1)S(1)} %arrange.1.refs_1_.refs_2_), channel_id=1, source_target_pairs={{0,4},{1,5},{2,6},{3,7},{4,0},{5,1},{6,2},{7,3},{8,12},{9,13},{10,... | collective-permute-start | bytes 4718600 | tf_op jit(solution)/shard_map/ppermute | solution.py:31
  30.4 21.1 %collective-permute-start.12 = (bf16[1,1,96,1024]{3,2,1,0:T(8,128)(2,1)S(1)}, bf16[1,1,96,1024]{3,2,1,0:T(8,128)(2,1)S(1)}, u32[]{:S(2)}, u32[]{:S(2)}) collective-permute-start(bf16[1,1,96,1024]{3,2,1,0:T(8,128)(2,1)S(1)} %slice.15), channel_id=1, source_target_pairs={{0,96},{1,97},{2,98},{3,99},{4,100},{5,101},{6,102},{7,103},{8,104... | collective-permute-start | bytes 589832 | tf_op jit(solution)/shard_map/ppermute | solution.py:31
  32.7 18.8 %collective-permute-start.11 = (bf16[1,1,96,1024]{3,2,1,0:T(8,128)(2,1)S(1)}, bf16[1,1,96,1024]{3,2,1,0:T(8,128)(2,1)S(1)}, u32[]{:S(2)}, u32[]{:S(2)}) collective-permute-start(bf16[1,1,96,1024]{3,2,1,0:T(8,128)(2,1)S(1)} %slice.14), channel_id=1, source_target_pairs={{0,32},{1,33},{2,34},{3,35},{4,36},{5,37},{6,38},{7,39},{8,40},{9,... | collective-permute-start | bytes 589832 | tf_op jit(solution)/shard_map/ppermute | solution.py:31
  49.4 24.2 %collective-permute-start.9 = (bf16[2,176,768]{2,1,0:T(8,128)(2,1)S(1)}, bf16[2,176,768]{2,1,0:T(8,128)(2,1)S(1)}, u32[]{:S(2)}, u32[]{:S(2)}) collective-permute-start(bf16[2,176,768]{2,1,0:T(8,128)(2,1)S(1)} %get-tuple-element.14), channel_id=1, source_target_pairs={{0,96},{1,97},{2,98},{3,99},{4,100},{5,101},{6,102},{7,103},{8,104... | collective-permute-start | bytes 1622024 | tf_op jit(solution)/shard_map/ppermute | solution.py:31
  49.5 15.4 %copy-start.2 = (bf16[1,2,96,1024]{3,2,1,0:T(8,128)(2,1)S(1)}, bf16[1,2,96,1024]{3,2,1,0:T(8,128)(2,1)}, u32[]{:S(2)}) copy-start(bf16[1,2,96,1024]{3,2,1,0:T(8,128)(2,1)} %refs_0_.1) | copy-start | bytes 1179652
  49.5 24.1 %collective-permute-start.10 = (bf16[2,176,768]{2,1,0:T(8,128)(2,1)S(1)}, bf16[2,176,768]{2,1,0:T(8,128)(2,1)S(1)}, u32[]{:S(2)}, u32[]{:S(2)}) collective-permute-start(bf16[2,176,768]{2,1,0:T(8,128)(2,1)S(1)} %get-tuple-element.15), channel_id=1, source_target_pairs={{0,32},{1,33},{2,34},{3,35},{4,36},{5,37},{6,38},{7,39},{8,40},{9,... | collective-permute-start | bytes 1622024 | tf_op jit(solution)/shard_map/ppermute | solution.py:31
  56.5 23.2 %collective-permute-start.13 = (bf16[2,176,768]{2,1,0:T(8,128)(2,1)S(1)}, bf16[2,176,768]{2,1,0:T(8,128)(2,1)S(1)}, u32[]{:S(2)}, u32[]{:S(2)}) collective-permute-start(bf16[2,176,768]{2,1,0:T(8,128)(2,1)S(1)} %attend.5), channel_id=1, source_target_pairs={{0,64},{1,65},{2,66},{3,67},{4,68},{5,69},{6,70},{7,71},{8,72},{9,... | collective-permute-start | bytes 1622024 | tf_op jit(solution)/shard_map/ppermute | solution.py:31
where the time goes:
time: 81.3 us; the launch traced here: 80.9 us
  Pallas kernels  34.8 us (43%)
  starting transfers between devices  26.8 us (33%)
  waiting for transfers between devices  14.3 us (18%)
  local copies, waits for them, and re-layouts  2.75 us (3%)
  other arithmetic  1.51 us (2%)
    pallas_call x3, Pallas kernels, attend(): pl.pallas_call(functools.partial(attend_kernel, q0, slots, diagonal), out...  29.3 us
    ppermute x14, starting transfers between devices, permute(): lax.ppermute(a, ('ctx', 'row'), [(device(*p), device(*target(*p))) for p...  26.8 us
    ppermute x14, waiting for transfers between devices, permute(): lax.ppermute(a, ('ctx', 'row'), [(device(*p), device(*target(*p))) for p...  14.3 us
    unnamed x7, local copies, waits for them, and re-layouts  2.69 us
    pallas_call x1, Pallas kernels, plan(): pl.pallas_call(plan_kernel, out_shape=jax.ShapeDtypeStruct((8, MAX_STEPS)...  2.48 us
    pallas_call x1, Pallas kernels, arrange(): pl.pallas_call(arrange_kernel, out_shape=jax.ShapeDtypeStruct((2 * NY, 2...  1.78 us
  transfers between devices with their start and end apart: 14, of which 5 were waited for; matrix products, arithmetic and copies ran while one was open for 3% of the time, Pallas kernels for 41%

commit v1 on v0

--- a/solution.py
+++ b/solution.py
@@ -74,8 +74,8 @@
     return ctx // (NY * NC), ctx // NC % NY, ctx % NC, lax.axis_index("row")
 
 
-def arrange_kernel(at, table, line, low, high, far_0, far_1, out_ref, vals):
-    y, core, z = at[1], at[2], at[3]
+def arrange_kernel(line, low, high, far_0, far_1, out_ref, vals):
+    _, y, core, z = place()
     here_1, here_2 = jnp.where(core == 0, y, z), jnp.where(core == 0, z, y)
     for i, di in enumerate(REL):
         for j, dj in enumerate(REL):
@@ -96,17 +96,17 @@
     lax.fori_loop(0, 2 * NY, turn, 0)
 
 
-def arrange(at, table, parts):
+def arrange(parts):
     vmem = pl.BlockSpec(memory_space=pltpu.VMEM)
     return pl.pallas_call(
         arrange_kernel,
         out_shape=jax.ShapeDtypeStruct((2 * NY, 2 * SPAN, HD), BF),
-        in_specs=[pl.BlockSpec(memory_space=pltpu.SMEM)] * 2 + [vmem] * 5,
+        in_specs=[vmem] * 5,
         out_specs=vmem,
         scratch_shapes=[pltpu.VMEM((2 * NY, SPAN, HD), BF)],
         compiler_params=pltpu.CompilerParams(vmem_limit_bytes=40 << 20),
         name="arrange",
-    )(at, table, *parts)
+    )(*parts)
 
 
 def attend_kernel(q0, slots, diagonal, table, *refs):
@@ -269,11 +269,11 @@
         safe = jnp.where(any_seen, total, 1.0)
         out = outs[tile // 2]
         out[tile % 2, :HD, :] = (acc[tile, :HD, :] * (1.0 / safe)).astype(BF)
-        left = jnp.broadcast_to(jnp.where(any_seen, ms[tile] * LN2 + jnp.log(safe), NEG), (16, TQ))
+        left, rows = jnp.where(any_seen, ms[tile] * LN2 + jnp.log(safe), NEG), []
         for part in range(3):
-            rounded = left.astype(BF)
-            out[tile % 2, HD + 16 * part : HD + 16 * part + 16, :] = rounded
-            left = left - rounded.astype(F32)
+            rows.append(left.astype(BF).astype(F32))
+            left = left - rows[-1]
+        out[tile % 2, HD:, :] = jnp.concatenate(rows + [jnp.zeros((13, TQ), F32)], axis=0).astype(BF)
 
 
 def attend(q0, slots, diagonal, table, queries, kv_own, kv_other):
@@ -284,7 +284,7 @@
     flops = 2 * groups * TQ * NK * SPAN * HD * 2
     return pl.pallas_call(
         functools.partial(attend_kernel, q0, slots, diagonal),
-        out_shape=[jax.ShapeDtypeStruct((2, HD + 48, TQ), BF)] * groups,
+        out_shape=[jax.ShapeDtypeStruct((2, HD + 16, TQ), BF)] * groups,
         in_specs=[pl.BlockSpec(memory_space=pltpu.SMEM)] + [hbm] * (len(queries) + 2),
         out_specs=[vmem] * groups,
         scratch_shapes=[
@@ -311,7 +311,7 @@
 def combine_kernel(*refs):
     parts, (out_ref, lse_ref) = refs[:4], refs[4:]
     for slot in range(2):
-        logs = [sum(r[slot, HD + 16 * p : HD + 16 * p + 1, :].astype(F32) for p in range(3)) for r in parts]
+        logs = [jnp.sum(r[slot, HD:, :].astype(F32), axis=0, keepdims=True) for r in parts]
         top = functools.reduce(jnp.maximum, logs)
         raw = [jnp.exp(v - top) for v in logs]
         total = sum(raw)
@@ -394,7 +394,8 @@
     line, low, high = gather_plane(near)
     from_low, from_high = shift_x(queries_next, 1), shift_x(queries_next, -1)
     far = shift_plane(line, 2, 1)
-    kv_own = arrange(at, table, (line, low, high, far[:2], far[2:]))
+    low, high, far, table = lax.optimization_barrier((low, high, far, table))
+    kv_own = arrange((line, low, high, far[:2], far[2:]))
     kv_own, from_low, from_high = lax.optimization_barrier((kv_own, from_low, from_high))
     kv_other = swap_core(kv_own)
     from_far = shift_x(from_low[:, :1], 1), shift_x(from_high[:, 1:], -1)

time: 81.3 us -> 78.6 us (0.967)
  Pallas kernels: 34.8 us -> 42.1 us
  waiting for transfers between devices: 14.3 us -> 10.1 us
  starting transfers between devices: 26.8 us -> 23 us
  local copies, waits for them, and re-layouts: 2.75 us -> 1.43 us
    pallas_call x3, Pallas kernels: 29.3 us -> 37 us  [attend(): pl.pallas_call(functools.partial(attend_kernel, q0, slots, diagonal), out...]
    ppermute x14, waiting for transfers between devices: 14.3 us -> 10.1 us  [permute(): lax.ppermute(a, ('ctx', 'row'), [(device(*p), device(*target(*p))) for p...]
    ppermute x14, starting transfers between devices: 26.8 us -> 23 us  [permute(): lax.ppermute(a, ('ctx', 'row'), [(device(*p), device(*target(*p))) for p...]
    unnamed x7 -> x5, local copies, waits for them, and re-layouts: 2.69 us -> 1.37 us
  transfers between devices with their start and end apart: 14 -> 14, of which waited for: 5 -> 4; matrix products, arithmetic and copies ran while one was open for 3% -> 3% of each run, Pallas kernels for 41% -> 52%
where the time goes in v1:
time: 78.6 us; the launch traced here: 78.9 us
  Pallas kernels  42.1 us (54%)
  starting transfers between devices  23 us (29%)
  waiting for transfers between devices  10.1 us (13%)
  other arithmetic  1.49 us (2%)
  local copies, waits for them, and re-layouts  1.43 us (2%)
    pallas_call x3, Pallas kernels, attend(): pl.pallas_call(functools.partial(attend_kernel, q0, slots, diagonal), out...  37 us
    ppermute x14, starting transfers between devices, permute(): lax.ppermute(a, ('ctx', 'row'), [(device(*p), device(*target(*p))) for p...  23 us
    ppermute x14, waiting for transfers between devices, permute(): lax.ppermute(a, ('ctx', 'row'), [(device(*p), device(*target(*p))) for p...  10.1 us
    pallas_call x1, Pallas kernels, plan(): pl.pallas_call(plan_kernel, out_shape=jax.ShapeDtypeStruct((8, MAX_STEPS)...  2.65 us
  transfers between devices with their start and end apart: 14, of which 4 were waited for; matrix products, arithmetic and copies ran while one was open for 3% of the time, Pallas kernels for 52%

profile of v1, /device:TPU:0, one launch (start us, length us, event | category | flops | bytes accessed | tf_op | source)
XLA Modules:
  0.0 78.9 jit_solution(7010889185466232957)
XLA Ops:
  0.6 0.8 %fusion = (bf16[1,2,96,256]{3,2,1,0:T(8,128)(2,1)S(1)}, bf16[2,96,256]{2,1,0:T(8,128)(2,1)S(1)}) fusion(bf16[2,96,128]{2,1,0:T(8,128)(2,1)} %bitcast.14, bf16[2,96,128]{2,1,0:T(8,128)(2,1)} %bitcast.15), kind=kLoop, calls=%fused_computation.3 | loop fusion | flops 196608 | bytes 294912 | tf_op jit(solution)/shard_map/stack | solution.py:61
  1.5 3.2 %collective-permute-start.1 = (bf16[2,96,256]{2,1,0:T(8,128)(2,1)S(1)}, bf16[2,96,256]{2,1,0:T(8,128)(2,1)S(1)}, u32[]{:S(2)}, u32[]{:S(2)}) collective-permute-start(bf16[2,96,256]{2,1,0:T(8,128)(2,1)S(1)} %get-tuple-element.27), channel_id=1, source_target_pairs={{0,24},{1,25},{2,26},{3,27},{4,7},{5,4},{6,5},{7,6},{8,0},{9,1},{1... | collective-permute-start | bytes 294920 | tf_op jit(solution)/shard_map/ppermute | solution.py:31
  4.6 2.2 %collective-permute-start.2 = (bf16[2,96,256]{2,1,0:T(8,128)(2,1)S(1)}, bf16[2,96,256]{2,1,0:T(8,128)(2,1)S(1)}, u32[]{:S(2)}, u32[]{:S(2)}) collective-permute-start(bf16[2,96,256]{2,1,0:T(8,128)(2,1)S(1)} %get-tuple-element.27), channel_id=1, source_target_pairs={{0,16},{1,17},{2,18},{3,19},{4,6},{5,7},{6,4},{7,5},{8,24},{9,25},... | collective-permute-start | bytes 294920 | tf_op jit(solution)/shard_map/ppermute | solution.py:31
  6.8 0.0 collective-permute-done.1
  6.9 4.7 %collective-permute-done = bf16[2,96,256]{2,1,0:T(8,128)(2,1)S(1)} collective-permute-done((bf16[2,96,256]{2,1,0:T(8,128)(2,1)S(1)}, bf16[2,96,256]{2,1,0:T(8,128)(2,1)S(1)}, u32[]{:S(2)}, u32[]{:S(2)}) %collective-permute-start) | collective-permute-done | bytes 98336 | tf_op jit(solution)/shard_map/ppermute | solution.py:31
  11.5 0.0 collective-permute-done.2
  11.5 0.1 pad_maximum_fusion.line
  11.6 4.0 %collective-permute-start.5 = (bf16[4,2,96,256]{3,2,1,0:T(8,128)(2,1)S(1)}, bf16[4,2,96,256]{3,2,1,0:T(8,128)(2,1)S(1)}, u32[]{:S(2)}, u32[]{:S(2)}) collective-permute-start(bf16[4,2,96,256]{3,2,1,0:T(8,128)(2,1)S(1)} %pad_maximum_fusion.line), channel_id=1, source_target_pairs={{0,2},{1,3},{2,0},{3,1},{4,20},{5,21},{6,22},{7,23},{8,10},{9,11},... | collective-permute-start | bytes 1179656 | tf_op jit(solution)/shard_map/ppermute | solution.py:31
  15.5 0.7 collective-permute-start.4
  16.2 1.3 %collective-permute-start.3 = (bf16[4,2,96,256]{3,2,1,0:T(8,128)(2,1)S(1)}, bf16[4,2,96,256]{3,2,1,0:T(8,128)(2,1)S(1)}, u32[]{:S(2)}, u32[]{:S(2)}) collective-permute-start(bf16[4,2,96,256]{3,2,1,0:T(8,128)(2,1)S(1)} %pad_maximum_fusion.line), channel_id=1, source_target_pairs={{0,1},{1,2},{2,3},{3,0},{4,12},{5,13},{6,14},{7,15},{8,9},{9,10},{... | collective-permute-start | bytes 1179656 | tf_op jit(solution)/shard_map/ppermute | solution.py:31
  17.6 2.8 %collective-permute-start.7 = (bf16[1,2,96,1024]{3,2,1,0:T(8,128)(2,1)}, bf16[1,2,96,1024]{3,2,1,0:T(8,128)(2,1)S(1)}, u32[]{:S(2)}, u32[]{:S(2)}) collective-permute-start(bf16[1,2,96,1024]{3,2,1,0:T(8,128)(2,1)} %refs_0_.1), channel_id=1, source_target_pairs={{0,96},{1,97},{2,98},{3,99},{4,100},{5,101},{6,102},{7,103},{8,104... | collective-permute-start | bytes 1179656 | tf_op jit(solution)/shard_map/ppermute | solution.py:31
  20.3 0.0 collective-permute-start.6
  20.3 1.4 %copy.6.assignment = s32[32,2]{1,0:T(8,128)} copy(s32[32,2]{0,1:T(2,128)} %param.7) | data formatting | bytes 512 | tf_op args[3]
  21.7 0.6 pad_add_fusion.at
  22.3 2.7 %plan.1.table = s32[8,72]{1,0:T(8,128)} custom-call(s32[4]{0:T(128)} %pad_add_fusion.at, s32[32,2]{1,0:T(8,128)} %copy.6.assignment), custom_call_target="tpu_custom_call" | custom-call | tf_op jit(solution)/shard_map/plan/pallas_call | solution.py:379
  24.9 0.0 collective-permute-done.5
  25.0 1.6 %collective-permute-done.4.high = bf16[4,2,96,256]{3,2,1,0:T(8,128)(2,1)S(1)} collective-permute-done((bf16[4,2,96,256]{3,2,1,0:T(8,128)(2,1)S(1)}, bf16[4,2,96,256]{3,2,1,0:T(8,128)(2,1)S(1)}, u32[]{:S(2)}, u32[]{:S(2)}) %collective-permute-start.4) | collective-permute-done | bytes 393248 | tf_op jit(solution)/shard_map/ppermute | solution.py:31
  26.6 0.0 collective-permute-done.3.low
  26.6 0.0 copy-start
  26.6 1.2 %arrange.1.refs_1_.refs_2_ = bf16[8,768,128]{2,1,0:T(8,128)(2,1)S(1)} custom-call(bf16[4,2,96,256]{3,2,1,0:T(8,128)(2,1)S(1)} %pad_maximum_fusion.line, bf16[4,2,96,256]{3,2,1,0:T(8,128)(2,1)S(1)} %collective-permute-done.3.low, bf16[4,2,96,256]{3,2,1,0:T(8,128)(2,1)S(1)} %collective-permute-done.4.high, ...), custom_call_target="tpu_custom_call" | custom-call | tf_op jit(solution)/shard_map/arrange/pallas_call | solution.py:101
  27.8 2.6 %collective-permute-done.6.refs_0_ = bf16[1,2,96,1024]{3,2,1,0:T(8,128)(2,1)S(1)} collective-permute-done((bf16[1,2,96,1024]{3,2,1,0:T(8,128)(2,1)}, bf16[1,2,96,1024]{3,2,1,0:T(8,128)(2,1)S(1)}, u32[]{:S(2)}, u32[]{:S(2)}) %collective-permute-start.6) | collective-permute-done | bytes 393248 | tf_op jit(solution)/shard_map/ppermute | solution.py:31
  30.4 0.0 collective-permute-start.8
  30.4 0.4 collective-permute-start.12
  30.8 1.7 %collective-permute-start.11 = (bf16[1,1,96,1024]{3,2,1,0:T(8,128)(2,1)S(1)}, bf16[1,1,96,1024]{3,2,1,0:T(8,128)(2,1)S(1)}, u32[]{:S(2)}, u32[]{:S(2)}) collective-permute-start(bf16[1,1,96,1024]{3,2,1,0:T(8,128)(2,1)S(1)} %slice.14), channel_id=1, source_target_pairs={{0,32},{1,33},{2,34},{3,35},{4,36},{5,37},{6,38},{7,39},{8,40},{9,... | collective-permute-start | bytes 589832 | tf_op jit(solution)/shard_map/ppermute | solution.py:31
  32.5 1.3 %collective-permute-done.8.refs_2_.refs_3_ = bf16[8,768,128]{2,1,0:T(8,128)(2,1)S(1)} collective-permute-done((bf16[8,768,128]{2,1,0:T(8,128)(2,1)S(1)}, bf16[8,768,128]{2,1,0:T(8,128)(2,1)S(1)}, u32[]{:S(2)}, u32[]{:S(2)}) %collective-permute-start.8) | collective-permute-done | bytes 1572896 | tf_op jit(solution)/shard_map/ppermute | solution.py:31
  33.8 16.2 %attend.4 = (bf16[2,144,768]{2,1,0:T(8,128)(2,1)S(1)}, bf16[2,144,768]{2,1,0:T(8,128)(2,1)S(1)}) custom-call(s32[8,72]{1,0:T(8,128)S(1)} %copy-done, bf16[1,2,96,1024]{3,2,1,0:T(8,128)(2,1)S(1)} %collective-permute-done.6.refs_0_, bf16[1,2,96,1024]{3,2,1,0:T(8,128)(2,1)S(1)} %collective-permute-done.7.refs_1_, ...), custom_call_target="tpu_custom_call" | custom-call | flops 4831838208 | bytes 6291456 | tf_op jit(solution)/shard_map/attend/pallas_call | solution.py:285
  50.0 2.2 %collective-permute-start.9 = (bf16[2,144,768]{2,1,0:T(8,128)(2,1)S(1)}, bf16[2,144,768]{2,1,0:T(8,128)(2,1)S(1)}, u32[]{:S(2)}, u32[]{:S(2)}) collective-permute-start(bf16[2,144,768]{2,1,0:T(8,128)(2,1)S(1)} %get-tuple-element.22), channel_id=1, source_target_pairs={{0,96},{1,97},{2,98},{3,99},{4,100},{5,101},{6,102},{7,103},{8,104... | collective-permute-start | bytes 1327112 | tf_op jit(solution)/shard_map/ppermute | solution.py:31
  52.2 0.8 %collective-permute-start.10 = (bf16[2,144,768]{2,1,0:T(8,128)(2,1)S(1)}, bf16[2,144,768]{2,1,0:T(8,128)(2,1)S(1)}, u32[]{:S(2)}, u32[]{:S(2)}) collective-permute-start(bf16[2,144,768]{2,1,0:T(8,128)(2,1)S(1)} %get-tuple-element.23), channel_id=1, source_target_pairs={{0,32},{1,33},{2,34},{3,35},{4,36},{5,37},{6,38},{7,39},{8,40},{9,... | collective-permute-start | bytes 1327112 | tf_op jit(solution)/shard_map/ppermute | solution.py:31
  53.0 9.1 %attend.5 = bf16[2,144,768]{2,1,0:T(8,128)(2,1)S(1)} custom-call(s32[8,72]{1,0:T(8,128)S(1)} %copy-done, bf16[1,1,96,1024]{3,2,1,0:T(8,128)(2,1)S(1)} %collective-permute-done.11.refs_0_, bf16[1,1,96,1024]{3,2,1,0:T(8,128)(2,1)S(1)} %collective-permute-done.12.refs_1_, bf16[8,768,128]{2,1,0:T(8,128)(2,1)S(1)} %arrange.1.refs_1_.refs_2_, ...), custom_call_target="tpu_custom_call" | custom-call | flops 2415919104 | bytes 6291456 | tf_op jit(solution)/shard_map/attend/pallas_call | solution.py:285
  62.2 3.7 %collective-permute-start.13 = (bf16[2,144,768]{2,1,0:T(8,128)(2,1)S(1)}, bf16[2,144,768]{2,1,0:T(8,128)(2,1)S(1)}, u32[]{:S(2)}, u32[]{:S(2)}) collective-permute-start(bf16[2,144,768]{2,1,0:T(8,128)(2,1)S(1)} %attend.5), channel_id=1, source_target_pairs={{0,64},{1,65},{2,66},{3,67},{4,68},{5,69},{6,70},{7,71},{8,72},{9,... | collective-permute-start | bytes 1327112 | tf_op jit(solution)/shard_map/ppermute | solution.py:31
  65.9 11.7 %attend.3.refs_0_ = bf16[2,144,768]{2,1,0:T(8,128)(2,1)S(1)} custom-call(s32[8,72]{1,0:T(8,128)S(1)} %copy-done, bf16[1,2,96,1024]{3,2,1,0:T(8,128)(2,1)S(1)} %copy-done.1, bf16[8,768,128]{2,1,0:T(8,128)(2,1)S(1)} %arrange.1.refs_1_.refs_2_, bf16[8,768,128]{2,1,0:T(8,128)(2,1)S(1)} %collective-permute-done.8.refs_2_.refs_3_), custom_call_target="tpu_custom_call" | custom-call | flops 2415919104 | bytes 6291456 | tf_op jit(solution)/shard_map/attend/pallas_call | solution.py:285
  77.6 1.3 %combine.1 = (bf16[1,2,96,1024]{3,2,1,0:T(8,128)(2,1)}, f32[1,2,8,96]{3,2,1,0:T(8,128)}) custom-call(bf16[2,144,768]{2,1,0:T(8,128)(2,1)S(1)} %attend.3.refs_0_, bf16[2,144,768]{2,1,0:T(8,128)(2,1)S(1)} %collective-permute-done.9.refs_1_, bf16[2,144,768]{2,1,0:T(8,128)(2,1)S(1)} %collective-permute-done.10.refs_2_, ...), custom_call_target="tpu_custom_call" | custom-call | tf_op jit(solution)/shard_map/combine/pallas_call | solution.py:328
  (13 shorter events, 0.1 us)
Async XLA Ops:
  1.5 5.4 %collective-permute-start.1 = (bf16[2,96,256]{2,1,0:T(8,128)(2,1)S(1)}, bf16[2,96,256]{2,1,0:T(8,128)(2,1)S(1)}, u32[]{:S(2)}, u32[]{:S(2)}) collective-permute-start(bf16[2,96,256]{2,1,0:T(8,128)(2,1)S(1)} %get-tuple-element.27), channel_id=1, source_target_pairs={{0,24},{1,25},{2,26},{3,27},{4,7},{5,4},{6,5},{7,6},{8,0},{9,1},{1... | collective-permute-start | bytes 294920 | tf_op jit(solution)/shard_map/ppermute | solution.py:31
  4.6 6.9 %collective-permute-start = (bf16[2,96,256]{2,1,0:T(8,128)(2,1)S(1)}, bf16[2,96,256]{2,1,0:T(8,128)(2,1)S(1)}, u32[]{:S(2)}, u32[]{:S(2)}) collective-permute-start(bf16[2,96,256]{2,1,0:T(8,128)(2,1)S(1)} %get-tuple-element.27), channel_id=1, source_target_pairs={{0,8},{1,9},{2,10},{3,11},{4,5},{5,6},{6,7},{7,4},{8,16},{9,17},{1... | collective-permute-start | bytes 294920 | tf_op jit(solution)/shard_map/ppermute | solution.py:31
  4.6 6.9 %collective-permute-start.2 = (bf16[2,96,256]{2,1,0:T(8,128)(2,1)S(1)}, bf16[2,96,256]{2,1,0:T(8,128)(2,1)S(1)}, u32[]{:S(2)}, u32[]{:S(2)}) collective-permute-start(bf16[2,96,256]{2,1,0:T(8,128)(2,1)S(1)} %get-tuple-element.27), channel_id=1, source_target_pairs={{0,16},{1,17},{2,18},{3,19},{4,6},{5,7},{6,4},{7,5},{8,24},{9,25},... | collective-permute-start | bytes 294920 | tf_op jit(solution)/shard_map/ppermute | solution.py:31
  11.6 13.4 %collective-permute-start.5 = (bf16[4,2,96,256]{3,2,1,0:T(8,128)(2,1)S(1)}, bf16[4,2,96,256]{3,2,1,0:T(8,128)(2,1)S(1)}, u32[]{:S(2)}, u32[]{:S(2)}) collective-permute-start(bf16[4,2,96,256]{3,2,1,0:T(8,128)(2,1)S(1)} %pad_maximum_fusion.line), channel_id=1, source_target_pairs={{0,2},{1,3},{2,0},{3,1},{4,20},{5,21},{6,22},{7,23},{8,10},{9,11},... | collective-permute-start | bytes 1179656 | tf_op jit(solution)/shard_map/ppermute | solution.py:31
  15.5 11.0 %collective-permute-start.4 = (bf16[4,2,96,256]{3,2,1,0:T(8,128)(2,1)S(1)}, bf16[4,2,96,256]{3,2,1,0:T(8,128)(2,1)S(1)}, u32[]{:S(2)}, u32[]{:S(2)}) collective-permute-start(bf16[4,2,96,256]{3,2,1,0:T(8,128)(2,1)S(1)} %pad_maximum_fusion.line), channel_id=1, source_target_pairs={{0,3},{1,0},{2,1},{3,2},{4,28},{5,29},{6,30},{7,31},{8,11},{9,8},{... | collective-permute-start | bytes 1179656 | tf_op jit(solution)/shard_map/ppermute | solution.py:31
  16.2 10.3 %collective-permute-start.3 = (bf16[4,2,96,256]{3,2,1,0:T(8,128)(2,1)S(1)}, bf16[4,2,96,256]{3,2,1,0:T(8,128)(2,1)S(1)}, u32[]{:S(2)}, u32[]{:S(2)}) collective-permute-start(bf16[4,2,96,256]{3,2,1,0:T(8,128)(2,1)S(1)} %pad_maximum_fusion.line), channel_id=1, source_target_pairs={{0,1},{1,2},{2,3},{3,0},{4,12},{5,13},{6,14},{7,15},{8,9},{9,10},{... | collective-permute-start | bytes 1179656 | tf_op jit(solution)/shard_map/ppermute | solution.py:31
  17.6 10.2 %collective-permute-start.7 = (bf16[1,2,96,1024]{3,2,1,0:T(8,128)(2,1)}, bf16[1,2,96,1024]{3,2,1,0:T(8,128)(2,1)S(1)}, u32[]{:S(2)}, u32[]{:S(2)}) collective-permute-start(bf16[1,2,96,1024]{3,2,1,0:T(8,128)(2,1)} %refs_0_.1), channel_id=1, source_target_pairs={{0,96},{1,97},{2,98},{3,99},{4,100},{5,101},{6,102},{7,103},{8,104... | collective-permute-start | bytes 1179656 | tf_op jit(solution)/shard_map/ppermute | solution.py:31
  20.3 10.1 %collective-permute-start.6 = (bf16[1,2,96,1024]{3,2,1,0:T(8,128)(2,1)}, bf16[1,2,96,1024]{3,2,1,0:T(8,128)(2,1)S(1)}, u32[]{:S(2)}, u32[]{:S(2)}) collective-permute-start(bf16[1,2,96,1024]{3,2,1,0:T(8,128)(2,1)} %refs_0_.1), channel_id=1, source_target_pairs={{0,32},{1,33},{2,34},{3,35},{4,36},{5,37},{6,38},{7,39},{8,40},{9,... | collective-permute-start | bytes 1179656 | tf_op jit(solution)/shard_map/ppermute | solution.py:31
  26.6 7.2 %copy-start = (s32[8,72]{1,0:T(8,128)S(1)}, s32[8,72]{1,0:T(8,128)}, u32[]{:S(2)}) copy-start(s32[8,72]{1,0:T(8,128)} %plan.1.table) | copy-start | bytes 6916
  30.4 3.4 %collective-permute-start.8 = (bf16[8,768,128]{2,1,0:T(8,128)(2,1)S(1)}, bf16[8,768,128]{2,1,0:T(8,128)(2,1)S(1)}, u32[]{:S(2)}, u32[]{:S(2)}) collective-permute-start(bf16[8,768,128]{2,1,0:T(8,128)(2,1)S(1)} %arrange.1.refs_1_.refs_2_), channel_id=1, source_target_pairs={{0,4},{1,5},{2,6},{3,7},{4,0},{5,1},{6,2},{7,3},{8,12},{9,13},{10,... | collective-permute-start | bytes 4718600 | tf_op jit(solution)/shard_map/ppermute | solution.py:31
  30.4 22.6 %collective-permute-start.12 = (bf16[1,1,96,1024]{3,2,1,0:T(8,128)(2,1)S(1)}, bf16[1,1,96,1024]{3,2,1,0:T(8,128)(2,1)S(1)}, u32[]{:S(2)}, u32[]{:S(2)}) collective-permute-start(bf16[1,1,96,1024]{3,2,1,0:T(8,128)(2,1)S(1)} %slice.15), channel_id=1, source_target_pairs={{0,96},{1,97},{2,98},{3,99},{4,100},{5,101},{6,102},{7,103},{8,104... | collective-permute-start | bytes 589832 | tf_op jit(solution)/shard_map/ppermute | solution.py:31
  30.8 22.2 %collective-permute-start.11 = (bf16[1,1,96,1024]{3,2,1,0:T(8,128)(2,1)S(1)}, bf16[1,1,96,1024]{3,2,1,0:T(8,128)(2,1)S(1)}, u32[]{:S(2)}, u32[]{:S(2)}) collective-permute-start(bf16[1,1,96,1024]{3,2,1,0:T(8,128)(2,1)S(1)} %slice.14), channel_id=1, source_target_pairs={{0,32},{1,33},{2,34},{3,35},{4,36},{5,37},{6,38},{7,39},{8,40},{9,... | collective-permute-start | bytes 589832 | tf_op jit(solution)/shard_map/ppermute | solution.py:31
  50.0 27.6 %collective-permute-start.9 = (bf16[2,144,768]{2,1,0:T(8,128)(2,1)S(1)}, bf16[2,144,768]{2,1,0:T(8,128)(2,1)S(1)}, u32[]{:S(2)}, u32[]{:S(2)}) collective-permute-start(bf16[2,144,768]{2,1,0:T(8,128)(2,1)S(1)} %get-tuple-element.22), channel_id=1, source_target_pairs={{0,96},{1,97},{2,98},{3,99},{4,100},{5,101},{6,102},{7,103},{8,104... | collective-permute-start | bytes 1327112 | tf_op jit(solution)/shard_map/ppermute | solution.py:31
  52.2 13.7 %copy-start.1 = (bf16[1,2,96,1024]{3,2,1,0:T(8,128)(2,1)S(1)}, bf16[1,2,96,1024]{3,2,1,0:T(8,128)(2,1)}, u32[]{:S(2)}) copy-start(bf16[1,2,96,1024]{3,2,1,0:T(8,128)(2,1)} %refs_0_.1) | copy-start | bytes 1179652
  52.2 25.4 %collective-permute-start.10 = (bf16[2,144,768]{2,1,0:T(8,128)(2,1)S(1)}, bf16[2,144,768]{2,1,0:T(8,128)(2,1)S(1)}, u32[]{:S(2)}, u32[]{:S(2)}) collective-permute-start(bf16[2,144,768]{2,1,0:T(8,128)(2,1)S(1)} %get-tuple-element.23), channel_id=1, source_target_pairs={{0,32},{1,33},{2,34},{3,35},{4,36},{5,37},{6,38},{7,39},{8,40},{9,... | collective-permute-start | bytes 1327112 | tf_op jit(solution)/shard_map/ppermute | solution.py:31
  62.2 15.4 %collective-permute-start.13 = (bf16[2,144,768]{2,1,0:T(8,128)(2,1)S(1)}, bf16[2,144,768]{2,1,0:T(8,128)(2,1)S(1)}, u32[]{:S(2)}, u32[]{:S(2)}) collective-permute-start(bf16[2,144,768]{2,1,0:T(8,128)(2,1)S(1)} %attend.5), channel_id=1, source_target_pairs={{0,64},{1,65},{2,66},{3,67},{4,68},{5,69},{6,70},{7,71},{8,72},{9,... | collective-permute-start | bytes 1327112 | tf_op jit(solution)/shard_map/ppermute | solution.py:31

commit v2 on v1

--- a/solution.py
+++ b/solution.py
@@ -124,6 +124,12 @@
     ]
     for c in fetches + copies:
         c.start()
+    def clear():
+        acc[...] = jnp.zeros_like(acc)
+        ms[...] = jnp.full_like(ms, NEG)
+        p1[...] = jnp.zeros_like(p1)
+
+    clear()
     for t in range(nq):
         fetches[t].wait()
         full = raw[t].astype(F32) * SCALE
@@ -157,11 +163,6 @@
 
     def query_tile(i):
         return jnp.clip(entry(0, i) - q0, 0, nq - 1)
-
-    def clear():
-        acc[...] = jnp.zeros_like(acc)
-        ms[...] = jnp.full_like(ms, NEG)
-        p1[...] = jnp.zeros_like(p1)
 
     def column_tops(x):
         return [jnp.max(x[half * SPAN : (half + 1) * SPAN], axis=0, keepdims=True) for half in range(2)]
@@ -222,7 +223,6 @@
 
     row = jnp.zeros((1, TQ), F32)
     pairs = (steps + 1) // 2
-    clear()
     for t in range(nq):
         k = kv[jnp.clip(table[1, table[6, q0 + t]], 0, NK - 1), :HD, :]
         x = dot_t(jnp.concatenate([k, k], axis=1), qt[t])
@@ -341,8 +341,8 @@
 ORDER = (2, -1, 1, 0)
 
 
-def plan_kernel(at, assignment, table, order):
-    x, y, core, row = at[0], at[1], at[2], at[3]
+def plan_kernel(assignment, table, order):
+    x, y, core, row = place()
     keys = [
         assignment[(x * NY + i) * NC + c, slot] for c in (core, 1 - core) for i in range(NY) for slot in range(2)
     ]
@@ -374,21 +374,20 @@
     table[6, 10] = y * 2
 
 
-def plan(at, assignment):
+def plan(assignment):
     smem = pl.BlockSpec(memory_space=pltpu.SMEM)
     return pl.pallas_call(
         plan_kernel,
         out_shape=jax.ShapeDtypeStruct((8, MAX_STEPS), I32),
-        in_specs=[smem, smem],
+        in_specs=[smem],
         out_specs=smem,
         scratch_shapes=[pltpu.SMEM((NK,), I32)],
         name="plan",
-    )(at, assignment)
+    )(assignment)
 
 
 def local(queries, keys, values, assignment):
-    at = jnp.stack(place()).astype(I32)
-    table = plan(at, assignment)
+    table = plan(assignment)
     near = gather_line(jnp.concatenate([keys[0], values[0]], axis=-1))
     near, queries_next = lax.optimization_barrier((near, queries))
     line, low, high = gather_plane(near)

time: 78.6 us -> 79.1 us (level)
  the two profiles are of different devices: /device:TPU:0 before, /device:TPU:3 now
where the time goes in v2:
time: 79.1 us; the launch traced here: 78.3 us
  Pallas kernels  46.8 us (59%)
  starting transfers between devices  18.1 us (23%)
  waiting for transfers between devices  10.4 us (13%)
  local copies, waits for them, and re-layouts  1.43 us (2%)
  other arithmetic  0.89 us (1%)
    pallas_call x3, Pallas kernels, attend(): pl.pallas_call(functools.partial(attend_kernel, q0, slots, diagonal), out...  41.6 us
    ppermute x14, starting transfers between devices, permute(): lax.ppermute(a, ('ctx', 'row'), [(device(*p), device(*target(*p))) for p...  18.1 us
    ppermute x14, waiting for transfers between devices, permute(): lax.ppermute(a, ('ctx', 'row'), [(device(*p), device(*target(*p))) for p...  10.4 us
    pallas_call x1, Pallas kernels, plan(): pl.pallas_call(plan_kernel, out_shape=jax.ShapeDtypeStruct((8, MAX_STEPS)...  2.76 us
  transfers between devices with their start and end apart: 14, of which 5 were waited for; matrix products, arithmetic and copies ran while one was open for 2% of the time, Pallas kernels for 58%

profile of v2, /device:TPU:3, one launch (start us, length us, event | category | flops | bytes accessed | tf_op | source)
XLA Modules:
  0.0 78.3 jit_solution(2517211406756901064)
XLA Ops:
  0.6 0.8 %fusion = (bf16[1,2,96,256]{3,2,1,0:T(8,128)(2,1)S(1)}, bf16[2,96,256]{2,1,0:T(8,128)(2,1)S(1)}) fusion(bf16[2,96,128]{2,1,0:T(8,128)(2,1)} %bitcast.10, bf16[2,96,128]{2,1,0:T(8,128)(2,1)} %bitcast.11), kind=kLoop, calls=%fused_computation.2 | loop fusion | flops 196608 | bytes 294912 | tf_op jit(solution)/shard_map/stack | solution.py:61
  1.5 3.8 %collective-permute-start.1 = (bf16[2,96,256]{2,1,0:T(8,128)(2,1)S(1)}, bf16[2,96,256]{2,1,0:T(8,128)(2,1)S(1)}, u32[]{:S(2)}, u32[]{:S(2)}) collective-permute-start(bf16[2,96,256]{2,1,0:T(8,128)(2,1)S(1)} %get-tuple-element.27), channel_id=1, source_target_pairs={{0,24},{1,25},{2,26},{3,27},{4,7},{5,4},{6,5},{7,6},{8,0},{9,1},{1... | collective-permute-start | bytes 294920 | tf_op jit(solution)/shard_map/ppermute | solution.py:31
  5.3 1.3 %collective-permute-start.2 = (bf16[2,96,256]{2,1,0:T(8,128)(2,1)S(1)}, bf16[2,96,256]{2,1,0:T(8,128)(2,1)S(1)}, u32[]{:S(2)}, u32[]{:S(2)}) collective-permute-start(bf16[2,96,256]{2,1,0:T(8,128)(2,1)S(1)} %get-tuple-element.27), channel_id=1, source_target_pairs={{0,16},{1,17},{2,18},{3,19},{4,6},{5,7},{6,4},{7,5},{8,24},{9,25},... | collective-permute-start | bytes 294920 | tf_op jit(solution)/shard_map/ppermute | solution.py:31
  6.6 0.3 collective-permute-done.1
  6.9 4.4 %collective-permute-done = bf16[2,96,256]{2,1,0:T(8,128)(2,1)S(1)} collective-permute-done((bf16[2,96,256]{2,1,0:T(8,128)(2,1)S(1)}, bf16[2,96,256]{2,1,0:T(8,128)(2,1)S(1)}, u32[]{:S(2)}, u32[]{:S(2)}) %collective-permute-start) | collective-permute-done | bytes 98336 | tf_op jit(solution)/shard_map/ppermute | solution.py:31
  11.3 0.1 pad_maximum_fusion.line
  11.4 2.7 %collective-permute-start.5 = (bf16[4,2,96,256]{3,2,1,0:T(8,128)(2,1)S(1)}, bf16[4,2,96,256]{3,2,1,0:T(8,128)(2,1)S(1)}, u32[]{:S(2)}, u32[]{:S(2)}) collective-permute-start(bf16[4,2,96,256]{3,2,1,0:T(8,128)(2,1)S(1)} %pad_maximum_fusion.line), channel_id=1, source_target_pairs={{0,2},{1,3},{2,0},{3,1},{4,20},{5,21},{6,22},{7,23},{8,10},{9,11},... | collective-permute-start | bytes 1179656 | tf_op jit(solution)/shard_map/ppermute | solution.py:31
  14.1 0.8 collective-permute-start.4
  14.9 0.7 collective-permute-start.3
  15.6 0.3 collective-permute-start.7
  15.8 1.2 %collective-permute-start.6 = (bf16[1,2,96,1024]{3,2,1,0:T(8,128)(2,1)}, bf16[1,2,96,1024]{3,2,1,0:T(8,128)(2,1)S(1)}, u32[]{:S(2)}, u32[]{:S(2)}) collective-permute-start(bf16[1,2,96,1024]{3,2,1,0:T(8,128)(2,1)} %refs_0_.1), channel_id=1, source_target_pairs={{0,32},{1,33},{2,34},{3,35},{4,36},{5,37},{6,38},{7,39},{8,40},{9,... | collective-permute-start | bytes 1179656 | tf_op jit(solution)/shard_map/ppermute | solution.py:31
  17.0 1.4 %copy.6.assignment = s32[32,2]{1,0:T(8,128)} copy(s32[32,2]{0,1:T(2,128)} %param.7) | data formatting | bytes 512 | tf_op args[3]
  18.4 2.8 %plan.1.table = s32[8,72]{1,0:T(8,128)} custom-call(s32[32,2]{1,0:T(8,128)} %copy.6.assignment), custom_call_target="tpu_custom_call" | custom-call | tf_op jit(solution)/shard_map/plan/pallas_call | solution.py:379
  21.1 0.0 collective-permute-done.5
  21.2 3.2 %collective-permute-done.4.high = bf16[4,2,96,256]{3,2,1,0:T(8,128)(2,1)S(1)} collective-permute-done((bf16[4,2,96,256]{3,2,1,0:T(8,128)(2,1)S(1)}, bf16[4,2,96,256]{3,2,1,0:T(8,128)(2,1)S(1)}, u32[]{:S(2)}, u32[]{:S(2)}) %collective-permute-start.4) | collective-permute-done | bytes 393248 | tf_op jit(solution)/shard_map/ppermute | solution.py:31
  24.4 0.0 copy-start
  24.4 1.2 %arrange.1.refs_1_.refs_2_ = bf16[8,768,128]{2,1,0:T(8,128)(2,1)S(1)} custom-call(bf16[4,2,96,256]{3,2,1,0:T(8,128)(2,1)S(1)} %pad_maximum_fusion.line, bf16[4,2,96,256]{3,2,1,0:T(8,128)(2,1)S(1)} %collective-permute-done.3.low, bf16[4,2,96,256]{3,2,1,0:T(8,128)(2,1)S(1)} %collective-permute-done.4.high, ...), custom_call_target="tpu_custom_call" | custom-call | tf_op jit(solution)/shard_map/arrange/pallas_call | solution.py:101
  25.6 0.0 collective-permute-done.7.refs_1_
  25.6 0.0 collective-permute-done.6.refs_0_
  25.6 3.0 %collective-permute-start.8 = (bf16[8,768,128]{2,1,0:T(8,128)(2,1)S(1)}, bf16[8,768,128]{2,1,0:T(8,128)(2,1)S(1)}, u32[]{:S(2)}, u32[]{:S(2)}) collective-permute-start(bf16[8,768,128]{2,1,0:T(8,128)(2,1)S(1)} %arrange.1.refs_1_.refs_2_), channel_id=1, source_target_pairs={{0,4},{1,5},{2,6},{3,7},{4,0},{5,1},{6,2},{7,3},{8,12},{9,13},{10,... | collective-permute-start | bytes 4718600 | tf_op jit(solution)/shard_map/ppermute | solution.py:31
  28.6 2.7 %collective-permute-start.12 = (bf16[1,1,96,1024]{3,2,1,0:T(8,128)(2,1)S(1)}, bf16[1,1,96,1024]{3,2,1,0:T(8,128)(2,1)S(1)}, u32[]{:S(2)}, u32[]{:S(2)}) collective-permute-start(bf16[1,1,96,1024]{3,2,1,0:T(8,128)(2,1)S(1)} %slice.15), channel_id=1, source_target_pairs={{0,96},{1,97},{2,98},{3,99},{4,100},{5,101},{6,102},{7,103},{8,104... | collective-permute-start | bytes 589832 | tf_op jit(solution)/shard_map/ppermute | solution.py:31
  31.3 0.3 collective-permute-done.8.refs_2_.refs_3_
  31.6 18.1 %attend.4 = (bf16[2,144,768]{2,1,0:T(8,128)(2,1)S(1)}, bf16[2,144,768]{2,1,0:T(8,128)(2,1)S(1)}) custom-call(s32[8,72]{1,0:T(8,128)S(1)} %copy-done, bf16[1,2,96,1024]{3,2,1,0:T(8,128)(2,1)S(1)} %collective-permute-done.6.refs_0_, bf16[1,2,96,1024]{3,2,1,0:T(8,128)(2,1)S(1)} %collective-permute-done.7.refs_1_, ...), custom_call_target="tpu_custom_call" | custom-call | flops 4831838208 | bytes 6291456 | tf_op jit(solution)/shard_map/attend/pallas_call | solution.py:285
  49.7 0.1 collective-permute-start.9
  49.8 0.0 copy-start.1
  49.8 1.4 %collective-permute-start.10 = (bf16[2,144,768]{2,1,0:T(8,128)(2,1)S(1)}, bf16[2,144,768]{2,1,0:T(8,128)(2,1)S(1)}, u32[]{:S(2)}, u32[]{:S(2)}) collective-permute-start(bf16[2,144,768]{2,1,0:T(8,128)(2,1)S(1)} %get-tuple-element.23), channel_id=1, source_target_pairs={{0,32},{1,33},{2,34},{3,35},{4,36},{5,37},{6,38},{7,39},{8,40},{9,... | collective-permute-start | bytes 1327112 | tf_op jit(solution)/shard_map/ppermute | solution.py:31
  51.3 0.0 collective-permute-done.12.refs_1_
  51.3 12.2 %attend.5 = bf16[2,144,768]{2,1,0:T(8,128)(2,1)S(1)} custom-call(s32[8,72]{1,0:T(8,128)S(1)} %copy-done, bf16[1,1,96,1024]{3,2,1,0:T(8,128)(2,1)S(1)} %collective-permute-done.11.refs_0_, bf16[1,1,96,1024]{3,2,1,0:T(8,128)(2,1)S(1)} %collective-permute-done.12.refs_1_, bf16[8,768,128]{2,1,0:T(8,128)(2,1)S(1)} %arrange.1.refs_1_.refs_2_, ...), custom_call_target="tpu_custom_call" | custom-call | flops 2415919104 | bytes 6291456 | tf_op jit(solution)/shard_map/attend/pallas_call | solution.py:285
  63.5 0.1 collective-permute-start.13
  63.6 11.3 %attend.3.refs_0_ = bf16[2,144,768]{2,1,0:T(8,128)(2,1)S(1)} custom-call(s32[8,72]{1,0:T(8,128)S(1)} %copy-done, bf16[1,2,96,1024]{3,2,1,0:T(8,128)(2,1)S(1)} %copy-done.1, bf16[8,768,128]{2,1,0:T(8,128)(2,1)S(1)} %arrange.1.refs_1_.refs_2_, bf16[8,768,128]{2,1,0:T(8,128)(2,1)S(1)} %collective-permute-done.8.refs_2_.refs_3_), custom_call_target="tpu_custom_call" | custom-call | flops 2415919104 | bytes 6291456 | tf_op jit(solution)/shard_map/attend/pallas_call | solution.py:285
  74.9 2.2 %collective-permute-done.13.refs_3_ = bf16[2,144,768]{2,1,0:T(8,128)(2,1)S(1)} collective-permute-done((bf16[2,144,768]{2,1,0:T(8,128)(2,1)S(1)}, bf16[2,144,768]{2,1,0:T(8,128)(2,1)S(1)}, u32[]{:S(2)}, u32[]{:S(2)}) %collective-permute-start.13) | collective-permute-done | bytes 442400 | tf_op jit(solution)/shard_map/ppermute | solution.py:31
  77.1 1.3 %combine.1 = (bf16[1,2,96,1024]{3,2,1,0:T(8,128)(2,1)}, f32[1,2,8,96]{3,2,1,0:T(8,128)}) custom-call(bf16[2,144,768]{2,1,0:T(8,128)(2,1)S(1)} %attend.3.refs_0_, bf16[2,144,768]{2,1,0:T(8,128)(2,1)S(1)} %collective-permute-done.9.refs_1_, bf16[2,144,768]{2,1,0:T(8,128)(2,1)S(1)} %collective-permute-done.10.refs_2_, ...), custom_call_target="tpu_custom_call" | custom-call | tf_op jit(solution)/shard_map/combine/pallas_call | solution.py:328
  (12 shorter events, 0.1 us)
Async XLA Ops:
  1.5 5.5 %collective-permute-start.1 = (bf16[2,96,256]{2,1,0:T(8,128)(2,1)S(1)}, bf16[2,96,256]{2,1,0:T(8,128)(2,1)S(1)}, u32[]{:S(2)}, u32[]{:S(2)}) collective-permute-start(bf16[2,96,256]{2,1,0:T(8,128)(2,1)S(1)} %get-tuple-element.27), channel_id=1, source_target_pairs={{0,24},{1,25},{2,26},{3,27},{4,7},{5,4},{6,5},{7,6},{8,0},{9,1},{1... | collective-permute-start | bytes 294920 | tf_op jit(solution)/shard_map/ppermute | solution.py:31
  5.3 6.0 %collective-permute-start = (bf16[2,96,256]{2,1,0:T(8,128)(2,1)S(1)}, bf16[2,96,256]{2,1,0:T(8,128)(2,1)S(1)}, u32[]{:S(2)}, u32[]{:S(2)}) collective-permute-start(bf16[2,96,256]{2,1,0:T(8,128)(2,1)S(1)} %get-tuple-element.27), channel_id=1, source_target_pairs={{0,8},{1,9},{2,10},{3,11},{4,5},{5,6},{6,7},{7,4},{8,16},{9,17},{1... | collective-permute-start | bytes 294920 | tf_op jit(solution)/shard_map/ppermute | solution.py:31
  5.3 6.0 %collective-permute-start.2 = (bf16[2,96,256]{2,1,0:T(8,128)(2,1)S(1)}, bf16[2,96,256]{2,1,0:T(8,128)(2,1)S(1)}, u32[]{:S(2)}, u32[]{:S(2)}) collective-permute-start(bf16[2,96,256]{2,1,0:T(8,128)(2,1)S(1)} %get-tuple-element.27), channel_id=1, source_target_pairs={{0,16},{1,17},{2,18},{3,19},{4,6},{5,7},{6,4},{7,5},{8,24},{9,25},... | collective-permute-start | bytes 294920 | tf_op jit(solution)/shard_map/ppermute | solution.py:31
  11.4 9.8 %collective-permute-start.5 = (bf16[4,2,96,256]{3,2,1,0:T(8,128)(2,1)S(1)}, bf16[4,2,96,256]{3,2,1,0:T(8,128)(2,1)S(1)}, u32[]{:S(2)}, u32[]{:S(2)}) collective-permute-start(bf16[4,2,96,256]{3,2,1,0:T(8,128)(2,1)S(1)} %pad_maximum_fusion.line), channel_id=1, source_target_pairs={{0,2},{1,3},{2,0},{3,1},{4,20},{5,21},{6,22},{7,23},{8,10},{9,11},... | collective-permute-start | bytes 1179656 | tf_op jit(solution)/shard_map/ppermute | solution.py:31
  14.1 10.3 %collective-permute-start.4 = (bf16[4,2,96,256]{3,2,1,0:T(8,128)(2,1)S(1)}, bf16[4,2,96,256]{3,2,1,0:T(8,128)(2,1)S(1)}, u32[]{:S(2)}, u32[]{:S(2)}) collective-permute-start(bf16[4,2,96,256]{3,2,1,0:T(8,128)(2,1)S(1)} %pad_maximum_fusion.line), channel_id=1, source_target_pairs={{0,3},{1,0},{2,1},{3,2},{4,28},{5,29},{6,30},{7,31},{8,11},{9,8},{... | collective-permute-start | bytes 1179656 | tf_op jit(solution)/shard_map/ppermute | solution.py:31
  14.9 9.5 %collective-permute-start.3 = (bf16[4,2,96,256]{3,2,1,0:T(8,128)(2,1)S(1)}, bf16[4,2,96,256]{3,2,1,0:T(8,128)(2,1)S(1)}, u32[]{:S(2)}, u32[]{:S(2)}) collective-permute-start(bf16[4,2,96,256]{3,2,1,0:T(8,128)(2,1)S(1)} %pad_maximum_fusion.line), channel_id=1, source_target_pairs={{0,1},{1,2},{2,3},{3,0},{4,12},{5,13},{6,14},{7,15},{8,9},{9,10},{... | collective-permute-start | bytes 1179656 | tf_op jit(solution)/shard_map/ppermute | solution.py:31
  15.6 10.0 %collective-permute-start.7 = (bf16[1,2,96,1024]{3,2,1,0:T(8,128)(2,1)}, bf16[1,2,96,1024]{3,2,1,0:T(8,128)(2,1)S(1)}, u32[]{:S(2)}, u32[]{:S(2)}) collective-permute-start(bf16[1,2,96,1024]{3,2,1,0:T(8,128)(2,1)} %refs_0_.1), channel_id=1, source_target_pairs={{0,96},{1,97},{2,98},{3,99},{4,100},{5,101},{6,102},{7,103},{8,104... | collective-permute-start | bytes 1179656 | tf_op jit(solution)/shard_map/ppermute | solution.py:31
  15.8 9.8 %collective-permute-start.6 = (bf16[1,2,96,1024]{3,2,1,0:T(8,128)(2,1)}, bf16[1,2,96,1024]{3,2,1,0:T(8,128)(2,1)S(1)}, u32[]{:S(2)}, u32[]{:S(2)}) collective-permute-start(bf16[1,2,96,1024]{3,2,1,0:T(8,128)(2,1)} %refs_0_.1), channel_id=1, source_target_pairs={{0,32},{1,33},{2,34},{3,35},{4,36},{5,37},{6,38},{7,39},{8,40},{9,... | collective-permute-start | bytes 1179656 | tf_op jit(solution)/shard_map/ppermute | solution.py:31
  24.4 7.3 %copy-start = (s32[8,72]{1,0:T(8,128)S(1)}, s32[8,72]{1,0:T(8,128)}, u32[]{:S(2)}) copy-start(s32[8,72]{1,0:T(8,128)} %plan.1.table) | copy-start | bytes 6916
  25.6 6.0 %collective-permute-start.8 = (bf16[8,768,128]{2,1,0:T(8,128)(2,1)S(1)}, bf16[8,768,128]{2,1,0:T(8,128)(2,1)S(1)}, u32[]{:S(2)}, u32[]{:S(2)}) collective-permute-start(bf16[8,768,128]{2,1,0:T(8,128)(2,1)S(1)} %arrange.1.refs_1_.refs_2_), channel_id=1, source_target_pairs={{0,4},{1,5},{2,6},{3,7},{4,0},{5,1},{6,2},{7,3},{8,12},{9,13},{10,... | collective-permute-start | bytes 4718600 | tf_op jit(solution)/shard_map/ppermute | solution.py:31
  28.6 22.6 %collective-permute-start.12 = (bf16[1,1,96,1024]{3,2,1,0:T(8,128)(2,1)S(1)}, bf16[1,1,96,1024]{3,2,1,0:T(8,128)(2,1)S(1)}, u32[]{:S(2)}, u32[]{:S(2)}) collective-permute-start(bf16[1,1,96,1024]{3,2,1,0:T(8,128)(2,1)S(1)} %slice.15), channel_id=1, source_target_pairs={{0,96},{1,97},{2,98},{3,99},{4,100},{5,101},{6,102},{7,103},{8,104... | collective-permute-start | bytes 589832 | tf_op jit(solution)/shard_map/ppermute | solution.py:31
  31.3 19.9 %collective-permute-start.11 = (bf16[1,1,96,1024]{3,2,1,0:T(8,128)(2,1)S(1)}, bf16[1,1,96,1024]{3,2,1,0:T(8,128)(2,1)S(1)}, u32[]{:S(2)}, u32[]{:S(2)}) collective-permute-start(bf16[1,1,96,1024]{3,2,1,0:T(8,128)(2,1)S(1)} %slice.14), channel_id=1, source_target_pairs={{0,32},{1,33},{2,34},{3,35},{4,36},{5,37},{6,38},{7,39},{8,40},{9,... | collective-permute-start | bytes 589832 | tf_op jit(solution)/shard_map/ppermute | solution.py:31
  49.7 25.2 %collective-permute-start.9 = (bf16[2,144,768]{2,1,0:T(8,128)(2,1)S(1)}, bf16[2,144,768]{2,1,0:T(8,128)(2,1)S(1)}, u32[]{:S(2)}, u32[]{:S(2)}) collective-permute-start(bf16[2,144,768]{2,1,0:T(8,128)(2,1)S(1)} %get-tuple-element.22), channel_id=1, source_target_pairs={{0,96},{1,97},{2,98},{3,99},{4,100},{5,101},{6,102},{7,103},{8,104... | collective-permute-start | bytes 1327112 | tf_op jit(solution)/shard_map/ppermute | solution.py:31
  49.8 13.8 %copy-start.1 = (bf16[1,2,96,1024]{3,2,1,0:T(8,128)(2,1)S(1)}, bf16[1,2,96,1024]{3,2,1,0:T(8,128)(2,1)}, u32[]{:S(2)}) copy-start(bf16[1,2,96,1024]{3,2,1,0:T(8,128)(2,1)} %refs_0_.1) | copy-start | bytes 1179652
  49.8 25.1 %collective-permute-start.10 = (bf16[2,144,768]{2,1,0:T(8,128)(2,1)S(1)}, bf16[2,144,768]{2,1,0:T(8,128)(2,1)S(1)}, u32[]{:S(2)}, u32[]{:S(2)}) collective-permute-start(bf16[2,144,768]{2,1,0:T(8,128)(2,1)S(1)} %get-tuple-element.23), channel_id=1, source_target_pairs={{0,32},{1,33},{2,34},{3,35},{4,36},{5,37},{6,38},{7,39},{8,40},{9,... | collective-permute-start | bytes 1327112 | tf_op jit(solution)/shard_map/ppermute | solution.py:31
  63.5 13.6 %collective-permute-start.13 = (bf16[2,144,768]{2,1,0:T(8,128)(2,1)S(1)}, bf16[2,144,768]{2,1,0:T(8,128)(2,1)S(1)}, u32[]{:S(2)}, u32[]{:S(2)}) collective-permute-start(bf16[2,144,768]{2,1,0:T(8,128)(2,1)S(1)} %attend.5), channel_id=1, source_target_pairs={{0,64},{1,65},{2,66},{3,67},{4,68},{5,69},{6,70},{7,71},{8,72},{9,... | collective-permute-start | bytes 1327112 | tf_op jit(solution)/shard_map/ppermute | solution.py:31
